TPU v7x, 32 devices: a whole 2x2x4 slice. The times are simulated.
32 devices in a mesh: ctx: 16 (over z, y, core), tp: 2 (over x).
Axes of the slice: x: 2, y: 2, z: 4, core: 2. Of those that a mesh axis runs over, the one named last changes fastest.
Arguments:
- tokens: bfloat16 [6144, 3072], P('ctx', 'tp'), may hold values from -6 to 6
- queries: bfloat16 [6144, 2048], P('ctx', 'tp'), may hold values from -16 to 16
- key_rows: bfloat16 [6144, 2048], P('ctx', 'tp'), may hold values from -16 to 16
- value_rows: bfloat16 [6144, 2048], P('ctx', 'tp'), may hold values from -6 to 6
- clip_ids: int32 [6144], replicated, may hold values from 0 to 3, never falling along the last dimension, each value on 1 to 4608 neighbouring positions
- causal: int32 [4], replicated, may hold values 0 or 1
- modulation: float32 [3, 4, 3072], replicated, may hold values from -3 to 3
- w_mlp: bfloat16 [3072, 6144], P(None, 'tp'), may hold values from -0.109375 to 0.109375
- w_attn_out: bfloat16 [2048, 3072], P('tp'), may hold values from -1 to 1
- w_mlp_out: bfloat16 [6144, 3072], P('tp'), may hold values from -0.078125 to 0.078125
Outputs:
- mixed: float32 [6144, 3072], P(('ctx', 'tp'))
Inputs may be any that keep to these rules, and one draw needn't show every extreme that they name: `clip_ids`: clip numbers never fall along the tokens; each of the 4 clips has 1 to 4608 tokens and one has exactly 4608.
All inputs are finite; a program needn't handle non-finite values.
Results may differ from a plain program's by a relative error of at most 0.0065.
Values may be sent and summed in bfloat16 or wider, within the bound.
No kernel may reach another device: no remote copies, remote signals or barrier semaphores. Data moves between devices by JAX's collectives and lax.ppermute only.
A program may use at most 192 MiB of HBM per device.

v0:
```python
import math

import jax
import jax.numpy as jnp
from jax import lax
from jax.sharding import PartitionSpec as P

HD = 128


neg_large = -1e30
eps_norm = 1e-06


def per_token(clip_rows, table):
    onehot = (clip_rows[:, None] == jnp.arange(table.shape[0], dtype=jnp.int32)[None, :]).astype(
        jnp.float32
    )
    return jnp.dot(onehot, table, precision=lax.Precision.HIGHEST)


def causal_rows(clip_rows, causal):
    matches = clip_rows[:, None] == jnp.arange(causal.shape[0], dtype=jnp.int32)[None, :]
    return jnp.sum(jnp.where(matches, causal[None, :], 0), axis=1)


def visible(query_ids, query_pos, query_causal, key_ids, key_pos):
    same_clip = query_ids[:, None] == key_ids[None, :]
    earlier = key_pos[None, :] <= query_pos[:, None]
    return same_clip & ((query_causal[:, None] == 0) | earlier)


def attend(carry_state, query_tile, allowed, key_tile, value_tile, inverse_root):
    numerator, running_max, denominator = carry_state
    scores = (
        jnp.einsum("ihd,jhd->hij", query_tile, key_tile, preferred_element_type=jnp.float32)
        * inverse_root
    )
    scores = jnp.where(allowed[None], scores, neg_large)
    new_max = jnp.maximum(running_max, jnp.transpose(jnp.max(scores, axis=2)))
    weights = jnp.where(allowed[None], jnp.exp(scores - jnp.transpose(new_max)[:, :, None]), 0.0)
    rounded = weights.astype(jnp.bfloat16)
    factor = jnp.exp(running_max - new_max)
    numerator = numerator * factor[:, :, None] + jnp.einsum(
        "hij,jhd->ihd", rounded, value_tile, preferred_element_type=jnp.float32
    )
    denominator = denominator * factor + jnp.transpose(jnp.sum(rounded.astype(jnp.float32), axis=2))
    return (numerator, new_max, denominator)


def attend_some(carry_state, query_tile, allowed, key_tile, value_tile, inverse_root):
    return attend(carry_state, query_tile, allowed, key_tile, value_tile, inverse_root)


def per_device(
    tokens,
    queries,
    key_rows,
    value_rows,
    clip_ids,
    causal,
    modulation,
    w_mlp,
    w_attn_out,
    w_mlp_out,
):
    local_rows = queries.shape[0]
    heads_local = queries.shape[1] // HD
    inverse_root = 1.0 / math.sqrt(HD)
    tp_size = lax.axis_size("tp")
    first_row = lax.axis_index("ctx") * local_rows
    own_pos = first_row + jnp.arange(local_rows, dtype=jnp.int32)
    own_ids = lax.dynamic_slice_in_dim(clip_ids, first_row, local_rows)
    own_causal = causal_rows(own_ids, causal)
    own_query = queries.reshape(local_rows, heads_local, HD)
    start_state = (
        jnp.zeros((local_rows, heads_local, HD), jnp.float32),
        jnp.full((local_rows, heads_local), neg_large, jnp.float32),
        jnp.zeros((local_rows, heads_local), jnp.float32),
    )
    whole_rows = lax.all_gather(tokens, "tp", axis=1, tiled=True)
    token_values = whole_rows.astype(jnp.float32)
    row_mean = jnp.mean(token_values, axis=1, keepdims=True)
    centred = token_values - row_mean
    row_var = jnp.mean(centred * centred, axis=1, keepdims=True)
    normed = centred * lax.rsqrt(row_var + eps_norm)
    shift_rows = per_token(own_ids, modulation[0])
    scale_rows = per_token(own_ids, modulation[1])
    modulated = (normed * (1.0 + scale_rows) + shift_rows).astype(jnp.bfloat16)
    hidden = jax.nn.gelu(
        jnp.dot(modulated, w_mlp, preferred_element_type=jnp.float32), approximate=True
    ).astype(jnp.bfloat16)
    carry_state = start_state
    key_piece = lax.all_gather(key_rows, "ctx", axis=0, tiled=True)
    value_piece = lax.all_gather(value_rows, "ctx", axis=0, tiled=True)
    piece_rows = key_piece.shape[0]
    tile_rows = piece_rows
    tile_rows = local_rows * math.gcd(piece_rows // local_rows, 4)

    def one_tile(inner_state, tile_index):
        offset = tile_index * tile_rows
        key_tile = lax.dynamic_slice_in_dim(key_piece, offset, tile_rows, 0).reshape(
            tile_rows, heads_local, HD
        )
        value_tile = lax.dynamic_slice_in_dim(value_piece, offset, tile_rows, 0).reshape(
            tile_rows, heads_local, HD
        )
        key_pos = offset + jnp.arange(tile_rows, dtype=jnp.int32)
        key_ids = lax.dynamic_slice_in_dim(clip_ids, offset, tile_rows)
        allowed = visible(own_ids, own_pos, own_causal, key_ids, key_pos)
        return (
            attend_some(inner_state, own_query, allowed, key_tile, value_tile, inverse_root),
            None,
        )

    carry_state, _ = lax.scan(
        one_tile, carry_state, jnp.arange(piece_rows // tile_rows, dtype=jnp.int32)
    )
    numerator, running_max, denominator = carry_state
    attended = (
        (numerator / denominator[:, :, None])
        .astype(jnp.bfloat16)
        .reshape(local_rows, heads_local * HD)
    )
    share_rows = local_rows // tp_size
    branch = lax.psum_scatter(
        jnp.dot(attended, w_attn_out, preferred_element_type=jnp.float32)
        + jnp.dot(hidden, w_mlp_out, preferred_element_type=jnp.float32),
        "tp",
        scatter_dimension=0,
        tiled=True,
    )
    first_share = lax.axis_index("tp") * share_rows
    residual = lax.dynamic_slice_in_dim(token_values, first_share, share_rows, 0)
    gate_rows = lax.dynamic_slice_in_dim(
        per_token(own_ids, modulation[2]), first_share, share_rows, 0
    )
    return residual + gate_rows * branch


def solution(mesh):
    in_specs = (
        P("ctx", "tp"),
        P("ctx", "tp"),
        P("ctx", "tp"),
        P("ctx", "tp"),
        P(),
        P(),
        P(),
        P(None, "tp"),
        P("tp", None),
        P("tp", None),
    )
    out_specs = P(("ctx", "tp"), None)
    return jax.shard_map(
        per_device, mesh=mesh, in_specs=in_specs, out_specs=out_specs, check_vma=False
    )
```

profile of v0, /device:TPU:0, one launch (start us, length us, event | category | flops | bytes accessed | tf_op | source)
XLA Modules:
  0.0 515.4 jit_solution(7784278729293772765)
XLA Ops:
  17.9 29.8 %all-gather.4.cloned.1.call-done = bf16[384,3072]{1,0:T(8,128)(2,1)} async-done(((bf16[384,1536]{1,0:T(8,128)(2,1)}), bf16[384,3072]{1,0:T(8,128)(2,1)}) %all-gather.4.cloned.1.call-update) | async-done | bytes 2359312 | tf_op jit(solution)/shard_map/all_gather | solution.py:81
  52.4 6.8 %add_convert_fusion = bf16[384,3072]{1,0:T(8,128)(2,1)} fusion(f32[384,3072]{1,0:T(8,128)} %fusion.17, bf16[384,3072]{1,0:T(8,128)(2,1)S(1)} %copy-done, f32[384]{0:T(512)S(1)} %add_rsqrt_fusion, f32[384]{0:T(512)S(1)} %broadcast_multiply_fusion, f32[3,4,3072]{2,1,0:T(4,128)S(1)} %copy-done.4, s32[384]{0:T(512)S(1)} %dynamic_slice.23), kind=kOutput, calls=%fused_computation.26 | convolution fusion | flops 64882176 | bytes 9492480 | tf_op jit(solution)/shard_map/dot_general | solution.py:19
  59.2 94.7 %all-gather.6.cloned.1.call-done = bf16[6144,1024]{0,1:T(8,128)(2,1)} async-done(((bf16[384,1024]{0,1:T(8,128)(2,1)}), bf16[6144,1024]{0,1:T(8,128)(2,1)}) %all-gather.6.cloned.1.call-update) | async-done | bytes 12582928 | tf_op jit(solution)/shard_map/all_gather | solution.py:94
  153.9 104.3 %all-gather.8.cloned.1.call-done = bf16[6144,1024]{0,1:T(8,128)(2,1)} async-done(((bf16[384,1024]{0,1:T(8,128)(2,1)}), bf16[6144,1024]{0,1:T(8,128)(2,1)}) %all-gather.8.cloned.1.call-update) | async-done | bytes 12582928 | tf_op jit(solution)/shard_map/all_gather | solution.py:95
  258.2 154.1 %while.15 = (s32[]{:T(128)}, f32[384,8,128]{0,2,1:T(8,128)S(1)}, f32[384,8]{0,1:T(8,128)S(1)}, f32[384,8]{0,1:T(8,128)S(1)}, s32[384]{0:T(512)S(1)}, /*index=5*/...) while((s32[]{:T(128)}, f32[384,8,128]{0,2,1:T(8,128)S(1)}, ...), condition=%wide.region_4.5_spmd.clone, body=%wide.region_1.4_spmd.clone.sunk | while | flops 2490254592 | bytes 82023400 | solution.py:116
  266.4 8.7 %fusion.49 = (f32[8,384]{1,0:T(8,128)S(1)}, f32[8,1536,384]{2,1,0:T(8,128)}) fusion(pred[384,1536]{0,1:T(8,128)(4,1)S(1)} %or_and_fusion.2, bf16[1536,8,128]{0,2,1:T(8,128)(2,1)S(1)} %bitcast.64, bf16[384,8,128]{2,0,1:T(8,128)(2,1)S(1)} %get-tuple-element.292), kind=kOutput, calls=%fused_computation.4.clone.1 | convolution fusion | flops 1222112256 | bytes 23408640 | tf_op jit(solution)/shard_map/while/body/eval_jaxpr/ihd,jhd->hij/dot_general | solution.py:36
  275.1 10.9 %convert_reduce_fusion.3 = f32[8,384]{1,0:T(8,128)S(1)} fusion(f32[8,384]{1,0:T(8,128)S(1)} %bitcast.66, f32[8,1536,384]{2,1,0:T(8,128)} %get-tuple-element.248, pred[384,1536]{0,1:T(8,128)(4,1)S(1)} %or_and_fusion.2), kind=kLoop, calls=%fused_computation.2.clone.1 | loop fusion | flops 33027072 | bytes 19488768 | tf_op jit(solution)/shard_map/while/body/eval_jaxpr/reduce_sum | solution.py:47
  286.0 10.7 %bitcast_add_fusion.5 = f32[384,8,128]{0,2,1:T(8,128)S(1)} fusion(f32[384,8,128]{0,2,1:T(8,128)S(1)} %get-tuple-element.268, bf16[1536,8,128]{0,2,1:T(8,128)(2,1)} %bitcast.65, f32[384,8]{0,1:T(8,128)S(1)} %get-tuple-element.249, pred[]{:T(512)S(6)} %compare.3, f32[8,1536,384]{2,1,0:T(8,128)} %get-tuple-element.248, f32[8,384]{1,0:T(8,128)S(1)} %bitcast.67, ...), kind=kOutput, calls=%fused_computation.6.clone.1 | convolution fusion | flops 1232732160 | bytes 25780224 | tf_op jit(solution)/shard_map/while/body/eval_jaxpr/hij,jhd->ihd/dot_general | solution.py:44
  299.9 5.0 constant_dynamic-slice_fusion.3
  304.9 8.7 %fusion.49 = (f32[8,384]{1,0:T(8,128)S(1)}, f32[8,1536,384]{2,1,0:T(8,128)}) fusion(pred[384,1536]{0,1:T(8,128)(4,1)S(1)} %or_and_fusion.2, bf16[1536,8,128]{0,2,1:T(8,128)(2,1)S(1)} %bitcast.64, bf16[384,8,128]{2,0,1:T(8,128)(2,1)S(1)} %get-tuple-element.292), kind=kOutput, calls=%fused_computation.4.clone.1 | convolution fusion | flops 1222112256 | bytes 23408640 | tf_op jit(solution)/shard_map/while/body/eval_jaxpr/ihd,jhd->hij/dot_general | solution.py:36
  313.6 10.9 %convert_reduce_fusion.3 = f32[8,384]{1,0:T(8,128)S(1)} fusion(f32[8,384]{1,0:T(8,128)S(1)} %bitcast.66, f32[8,1536,384]{2,1,0:T(8,128)} %get-tuple-element.248, pred[384,1536]{0,1:T(8,128)(4,1)S(1)} %or_and_fusion.2), kind=kLoop, calls=%fused_computation.2.clone.1 | loop fusion | flops 33027072 | bytes 19488768 | tf_op jit(solution)/shard_map/while/body/eval_jaxpr/reduce_sum | solution.py:47
  324.5 10.7 %bitcast_add_fusion.5 = f32[384,8,128]{0,2,1:T(8,128)S(1)} fusion(f32[384,8,128]{0,2,1:T(8,128)S(1)} %get-tuple-element.268, bf16[1536,8,128]{0,2,1:T(8,128)(2,1)} %bitcast.65, f32[384,8]{0,1:T(8,128)S(1)} %get-tuple-element.249, pred[]{:T(512)S(6)} %compare.3, f32[8,1536,384]{2,1,0:T(8,128)} %get-tuple-element.248, f32[8,384]{1,0:T(8,128)S(1)} %bitcast.67, ...), kind=kOutput, calls=%fused_computation.6.clone.1 | convolution fusion | flops 1232732160 | bytes 25780224 | tf_op jit(solution)/shard_map/while/body/eval_jaxpr/hij,jhd->ihd/dot_general | solution.py:44
  338.4 5.0 constant_dynamic-slice_fusion.3
  343.4 8.7 %fusion.49 = (f32[8,384]{1,0:T(8,128)S(1)}, f32[8,1536,384]{2,1,0:T(8,128)}) fusion(pred[384,1536]{0,1:T(8,128)(4,1)S(1)} %or_and_fusion.2, bf16[1536,8,128]{0,2,1:T(8,128)(2,1)S(1)} %bitcast.64, bf16[384,8,128]{2,0,1:T(8,128)(2,1)S(1)} %get-tuple-element.292), kind=kOutput, calls=%fused_computation.4.clone.1 | convolution fusion | flops 1222112256 | bytes 23408640 | tf_op jit(solution)/shard_map/while/body/eval_jaxpr/ihd,jhd->hij/dot_general | solution.py:36
  352.1 10.9 %convert_reduce_fusion.3 = f32[8,384]{1,0:T(8,128)S(1)} fusion(f32[8,384]{1,0:T(8,128)S(1)} %bitcast.66, f32[8,1536,384]{2,1,0:T(8,128)} %get-tuple-element.248, pred[384,1536]{0,1:T(8,128)(4,1)S(1)} %or_and_fusion.2), kind=kLoop, calls=%fused_computation.2.clone.1 | loop fusion | flops 33027072 | bytes 19488768 | tf_op jit(solution)/shard_map/while/body/eval_jaxpr/reduce_sum | solution.py:47
  363.0 10.7 %bitcast_add_fusion.5 = f32[384,8,128]{0,2,1:T(8,128)S(1)} fusion(f32[384,8,128]{0,2,1:T(8,128)S(1)} %get-tuple-element.268, bf16[1536,8,128]{0,2,1:T(8,128)(2,1)} %bitcast.65, f32[384,8]{0,1:T(8,128)S(1)} %get-tuple-element.249, pred[]{:T(512)S(6)} %compare.3, f32[8,1536,384]{2,1,0:T(8,128)} %get-tuple-element.248, f32[8,384]{1,0:T(8,128)S(1)} %bitcast.67, ...), kind=kOutput, calls=%fused_computation.6.clone.1 | convolution fusion | flops 1232732160 | bytes 25780224 | tf_op jit(solution)/shard_map/while/body/eval_jaxpr/hij,jhd->ihd/dot_general | solution.py:44
  381.9 8.7 %fusion.49 = (f32[8,384]{1,0:T(8,128)S(1)}, f32[8,1536,384]{2,1,0:T(8,128)}) fusion(pred[384,1536]{0,1:T(8,128)(4,1)S(1)} %or_and_fusion.2, bf16[1536,8,128]{0,2,1:T(8,128)(2,1)S(1)} %bitcast.64, bf16[384,8,128]{2,0,1:T(8,128)(2,1)S(1)} %get-tuple-element.292), kind=kOutput, calls=%fused_computation.4.clone.1 | convolution fusion | flops 1222112256 | bytes 23408640 | tf_op jit(solution)/shard_map/while/body/eval_jaxpr/ihd,jhd->hij/dot_general | solution.py:36
  390.5 10.9 %convert_reduce_fusion.3 = f32[8,384]{1,0:T(8,128)S(1)} fusion(f32[8,384]{1,0:T(8,128)S(1)} %bitcast.66, f32[8,1536,384]{2,1,0:T(8,128)} %get-tuple-element.248, pred[384,1536]{0,1:T(8,128)(4,1)S(1)} %or_and_fusion.2), kind=kLoop, calls=%fused_computation.2.clone.1 | loop fusion | flops 33027072 | bytes 19488768 | tf_op jit(solution)/shard_map/while/body/eval_jaxpr/reduce_sum | solution.py:47
  401.5 10.7 %bitcast_add_fusion.5 = f32[384,8,128]{0,2,1:T(8,128)S(1)} fusion(f32[384,8,128]{0,2,1:T(8,128)S(1)} %get-tuple-element.268, bf16[1536,8,128]{0,2,1:T(8,128)(2,1)} %bitcast.65, f32[384,8]{0,1:T(8,128)S(1)} %get-tuple-element.249, pred[]{:T(512)S(6)} %compare.3, f32[8,1536,384]{2,1,0:T(8,128)} %get-tuple-element.248, f32[8,384]{1,0:T(8,128)S(1)} %bitcast.67, ...), kind=kOutput, calls=%fused_computation.6.clone.1 | convolution fusion | flops 1232732160 | bytes 25780224 | tf_op jit(solution)/shard_map/while/body/eval_jaxpr/hij,jhd->ihd/dot_general | solution.py:44
  412.5 7.9 %fusion.33 = f32[384,3072]{1,0:T(8,128)} fusion(bf16[384,1024]{0,1:T(8,128)(2,1)S(1)} %bitcast.68, bf16[1024,3072]{1,0:T(8,128)(2,1)} %param.20), kind=kOutput, calls=%fused_computation.56 | convolution fusion | flops 2415919104 | bytes 11796480 | tf_op jit(solution)/shard_map/dot_general | solution.py:127
  420.4 25.1 %convolution_add_fusion = f32[384,3072]{1,0:T(8,128)} fusion(f32[384,3072]{1,0:T(8,128)} %fusion.33, bf16[3072,3072]{1,0:T(8,128)(2,1)} %param.21, bf16[384,3072]{1,0:T(8,128)(2,1)S(1)} %copy-done.2, bf16[3072,3072]{1,0:T(8,128)(2,1)} %param.19), kind=kOutput, calls=%fused_computation.28 | convolution fusion | flops 14507311104 | bytes 49545216 | tf_op jit(solution)/shard_map/dot_general | solution.py:128
  445.5 5.4 %fusion.19 = f32[384,3072]{1,0:T(8,128)} fusion(f32[3,4,3072]{2,1,0:T(4,128)} %param.18, s32[384]{0:T(512)S(1)} %get-tuple-element.315), kind=kOutput, calls=%fused_computation.39 | convolution fusion | flops 56624640 | bytes 4769280 | tf_op jit(solution)/shard_map/dot_general | solution.py:19
  453.6 50.2 %reduce-scatter.2.cloned.1.call-done = f32[192,3072]{1,0:T(8,128)} async-done(((f32[384,3072]{1,0:T(8,128)}), f32[192,3072]{1,0:T(8,128)}) %reduce-scatter.2.cloned.1.call-update) | async-done | bytes 2359312 | tf_op jit(solution)/shard_map/reduce_scatter | solution.py:126
  503.8 5.1 multiply_add_fusion
  (75 shorter events, 39.1 us)
Async XLA Ops:
  6.5 5.5 %copy-start.3 = (bf16[384,1024]{1,0:T(8,128)(2,1)S(1)}, bf16[384,1024]{1,0:T(8,128)(2,1)}, u32[]{:S(2)}) copy-start(bf16[384,1024]{1,0:T(8,128)(2,1)} %param.13) | copy-start | bytes 2359300
  6.5 7.1 %copy-start.5 = (s32[4]{0:T(128)S(1)}, s32[4]{0:T(128)}, u32[]{:S(2)}) copy-start(s32[4]{0:T(128)} %param.17) | copy-start | bytes 52
  6.5 7.2 %copy-start.4 = (f32[3,4,3072]{2,1,0:T(4,128)S(1)}, f32[3,4,3072]{2,1,0:T(4,128)}, u32[]{:S(2)}) copy-start(f32[3,4,3072]{2,1,0:T(4,128)} %param.18) | copy-start | bytes 442372
  6.5 41.2 %all-gather.4.cloned.1.call-start = ((), (), s32[]{:S(2)}) async-start(), calls=%async_computation.1 | async-start | bytes 3538944 | tf_op jit(solution)/shard_map/all_gather | solution.py:81
  7.3 146.6 %all-gather.6.cloned.1.call-start = ((), (), s32[]{:S(2)}) async-start(), calls=%async_computation.2 | async-start | bytes 13369344 | tf_op jit(solution)/shard_map/all_gather | solution.py:94
  9.6 248.6 %all-gather.8.cloned.1.call-start = ((), (), s32[]{:S(2)}) async-start(), calls=%async_computation.3 | async-start | bytes 13369344 | tf_op jit(solution)/shard_map/all_gather | solution.py:95
  12.0 491.8 %reduce-scatter.2.cloned.1.call-start = ((), (), s32[]{:S(2)}) async-start(), calls=%async_computation.4 | async-start | bytes 7077888 | tf_op jit(solution)/shard_map/reduce_scatter | solution.py:126
  47.7 4.6 copy-start
  412.5 7.9 %copy-start.2 = (bf16[384,3072]{1,0:T(8,128)(2,1)S(1)}, bf16[384,3072]{1,0:T(8,128)(2,1)}, u32[]{:S(2)}) copy-start(bf16[384,3072]{1,0:T(8,128)(2,1)} %add_convert_fusion) | copy-start | bytes 7077892
  445.5 5.4 %copy-start.1 = (bf16[384,3072]{1,0:T(8,128)(2,1)S(1)}, bf16[384,3072]{1,0:T(8,128)(2,1)}, u32[]{:S(2)}) copy-start(bf16[384,3072]{1,0:T(8,128)(2,1)} %all-gather.4.cloned.1.call-done) | copy-start | bytes 7077892
Sparse Core Ops, SparseCore 0:
  8.9 38.7 all-gather.3
  49.9 103.9 all-gather.5
  156.0 102.1 all-gather.7
  445.6 58.1 reduce-scatter.1
where the time goes:
time: 516 us; the launch traced here: 515 us
  waiting for transfers between devices  280 us (54%)
  matrix products  127 us (25%)
  other arithmetic  60.9 us (12%)
  local copies, waits for them, and re-layouts  31.8 us (6%)
  between operations  13.2 us (3%)
    all_gather x1, waiting for transfers between devices, per_device(): value_piece = lax.all_gather(value_rows, 'ctx', axis=0, tiled=True)  104 us
    all_gather x1, waiting for transfers between devices, per_device(): key_piece = lax.all_gather(key_rows, 'ctx', axis=0, tiled=True)  94.7 us
    reduce_scatter x1, waiting for transfers between devices, per_device(): lax.psum_scatter(jnp.dot(attended, w_attn_out, preferred_element_type=jnp...  50.2 us
    reduce_sum x4, other arithmetic, attend(): jnp.sum(rounded.astype(jnp.float32), axis=2)  43.6 us
    dot_general x4, matrix products, attend(): jnp.einsum('hij,jhd->ihd', rounded, value_tile, preferred_element_type=jn...  42.6 us
    dot_general x4, matrix products, attend(): jnp.einsum('ihd,jhd->hij', query_tile, key_tile, preferred_element_type=j...  34.7 us
    all_gather x1, waiting for transfers between devices, per_device(): whole_rows = lax.all_gather(tokens, 'tp', axis=1, tiled=True)  29.8 us
    dot_general x1, matrix products, per_device(): jnp.dot(hidden, w_mlp_out, preferred_element_type=jnp.float32)  25.1 us
  transfers between devices with their start and end apart: 4, of which 4 were waited for; matrix products, arithmetic and copies ran while one was open for 6% of the time, Pallas kernels for 0%

commit v1 on v0

v1 whole, which is shorter than its diff:
```python
import functools
import math

import jax
import jax.numpy as jnp
from jax import lax
from jax.experimental import pallas as pl
from jax.experimental.pallas import tpu as pltpu
from jax.sharding import PartitionSpec as P

HD = 128
LANES = 128
ONES_ROWS = 8
MASKED = -3e38
START_MAX = -1e30
EPS_NORM = 1e-06
EXP2_SCALE = math.log2(math.e) / math.sqrt(HD)
VMEM_LIMIT = 48 << 20

ANY = pl.BlockSpec(memory_space=pl.ANY)
SMEM = pl.BlockSpec(memory_space=pltpu.SMEM)
VMEM = pl.BlockSpec(memory_space=pltpu.VMEM)


def params():
    return pltpu.CompilerParams(vmem_limit_bytes=VMEM_LIMIT)


def cost(flops, nbytes, exps=0):
    return pl.CostEstimate(flops=flops, bytes_accessed=nbytes, transcendentals=exps)


def split_kernel(chips, chip_ref, q_ref, k_ref, v_ref, *outs):
    rows = q_ref.shape[0]
    for k in range(chips):
        head = lax.bitwise_xor(chip_ref[0], k)
        columns = pl.ds(pl.multiple_of(head * HD, HD), HD)
        kv_out, q_out = outs[2 * k], outs[2 * k + 1]
        q_out[...] = q_ref[:, columns]
        kv_out[0] = k_ref[:, columns]
        for at in range(0, rows, LANES):
            block = v_ref[at : at + LANES, columns].astype(jnp.float32)
            kv_out[1, at : at + LANES, :] = jnp.transpose(block).astype(jnp.bfloat16)


def split_heads(chip, chips, queries, key_rows, value_rows):
    rows = queries.shape[0]
    shapes = []
    for _ in range(chips):
        shapes.append(jax.ShapeDtypeStruct((2, rows, HD), jnp.bfloat16))
        shapes.append(jax.ShapeDtypeStruct((rows, HD), jnp.bfloat16))
    outs = pl.pallas_call(
        functools.partial(split_kernel, chips),
        out_shape=shapes,
        in_specs=[SMEM, VMEM, VMEM, VMEM],
        out_specs=[VMEM] * len(shapes),
        compiler_params=params(),
        name="split_heads",
    )(chip[None], queries, key_rows, value_rows)
    return outs[0::2], outs[1::2]


def span_of(scalars, clips, pos):
    low = jnp.zeros_like(pos)
    high = jnp.zeros_like(pos)
    for clip in range(clips):
        inside = pos >= scalars[clip]
        end = jnp.where(scalars[clips + 1 + clip] != 0, pos + 1, scalars[clip + 1])
        low = jnp.where(inside, scalars[clip], low)
        high = jnp.where(inside, end, high)
    return low, high


def attention_kernel(clips, n_query, n_kv, key_tile, scalars, *refs):
    query_hbm = refs[:n_query]
    kv_hbm = refs[n_query : n_query + n_kv]
    out_hbm = refs[n_query + n_kv : 2 * n_query + n_kv]
    q, k, v, out, total, peak, score_a, score_b, block_peak, sems = refs[2 * n_query + n_kv :]
    rows = q.shape[1]
    all_keys = k.shape[0]
    query_at = 2 * clips + 1
    kv_at = query_at + n_query
    copies = []
    for i in range(n_query):
        copies.append(pltpu.make_async_copy(query_hbm[i], q.at[i], sems.at[len(copies)]))
    for i in range(n_kv):
        count = kv_hbm[i].shape[1]
        base = pl.multiple_of(scalars[kv_at + i], LANES)
        copies.append(
            pltpu.make_async_copy(kv_hbm[i].at[0], k.at[pl.ds(base, count)], sems.at[len(copies)])
        )
        for at in range(0, count, LANES):
            copies.append(
                pltpu.make_async_copy(
                    kv_hbm[i].at[1, at : at + LANES],
                    v.at[0:HD, pl.ds(pl.multiple_of(base + at, LANES), LANES)],
                    sems.at[len(copies)],
                )
            )
    for copy in copies:
        copy.start()
    v[HD:, :] = jnp.ones((ONES_ROWS, all_keys), jnp.bfloat16)
    for copy in copies:
        copy.wait()
    scores = [score_a, score_b]

    def one_piece(piece, _):
        base = scalars[query_at + piece]
        low_first, high_first = span_of(scalars, clips, base)
        low_last, high_last = span_of(scalars, clips, base + rows - 1)
        begin = low_first // key_tile
        end = (high_last + key_tile - 1) // key_tile
        full_from = (low_last + key_tile - 1) // key_tile
        full_to = high_first // key_tile
        pos = base + lax.broadcasted_iota(jnp.int32, (1, rows), 1)
        low, high = span_of(scalars, clips, pos)
        total[...] = jnp.zeros_like(total)
        peak[...] = jnp.full_like(peak, START_MAX)

        def multiply(tile, slot):
            keys = k[pl.ds(pl.multiple_of(tile * key_tile, key_tile), key_tile), :]
            block = lax.dot_general(
                keys, q[piece], (((1,), (1,)), ((), ())), preferred_element_type=jnp.float32
            )
            scores[slot][...] = block
            block_peak[slot] = jnp.max(block, axis=0, keepdims=True)

        def mask(tile, slot):
            @pl.when((tile < full_from) | (tile >= full_to))
            def _():
                key_pos = tile * key_tile + lax.broadcasted_iota(jnp.int32, (key_tile, 1), 0)
                allowed = (key_pos >= low) & (key_pos < high)
                block = jnp.where(allowed, scores[slot][...], MASKED)
                scores[slot][...] = block
                block_peak[slot] = jnp.max(block, axis=0, keepdims=True)

        def gather(tile, slot):
            old = peak[...]
            new = jnp.maximum(old, block_peak[slot])
            peak[...] = new
            factor = jnp.exp2((old - new) * EXP2_SCALE)
            weights = jnp.exp2(scores[slot][...] * EXP2_SCALE - new * EXP2_SCALE)
            values = v[:, pl.ds(pl.multiple_of(tile * key_tile, key_tile), key_tile)]
            total[...] = total[...] * factor + jnp.dot(
                values, weights.astype(jnp.bfloat16), preferred_element_type=jnp.float32
            )

        multiply(begin, 0)
        mask(begin, 0)
        count = end - begin

        def two_tiles(pair, _):
            tile = begin + 2 * pair
            multiply(tile + 1, 1)
            gather(tile, 0)
            mask(tile + 1, 1)
            later = jnp.minimum(tile + 2, end - 1)
            multiply(later, 0)
            gather(tile + 1, 1)
            mask(later, 0)
            return 0

        lax.fori_loop(0, count // 2, two_tiles, 0)

        @pl.when(count % 2 == 1)
        def _():
            gather(end - 1, 0)

        both = total[...]
        out[piece] = jnp.transpose(both[:HD] / both[HD : HD + 1]).astype(jnp.bfloat16)
        return 0

    lax.fori_loop(0, n_query, one_piece, 0)
    copies = [
        pltpu.make_async_copy(out.at[i], out_hbm[i], sems.at[i]) for i in range(n_query)
    ]
    for copy in copies:
        copy.start()
    for copy in copies:
        copy.wait()


def attention(clips, scalars, query_pieces, kv_pieces):
    rows = query_pieces[0].shape[0]
    n_query, n_kv = len(query_pieces), len(kv_pieces)
    all_keys = sum(piece.shape[1] for piece in kv_pieces)
    key_tile = math.gcd(all_keys, 768)
    n_sems = n_query + sum(1 + piece.shape[1] // LANES for piece in kv_pieces)
    return pl.pallas_call(
        functools.partial(attention_kernel, clips, n_query, n_kv, key_tile),
        out_shape=[jax.ShapeDtypeStruct((rows, HD), jnp.bfloat16)] * n_query,
        in_specs=[SMEM] + [ANY] * (n_query + n_kv),
        out_specs=[ANY] * n_query,
        scratch_shapes=[
            pltpu.VMEM((n_query, rows, HD), jnp.bfloat16),
            pltpu.VMEM((all_keys, HD), jnp.bfloat16),
            pltpu.VMEM((HD + ONES_ROWS, all_keys), jnp.bfloat16),
            pltpu.VMEM((n_query, rows, HD), jnp.bfloat16),
            pltpu.VMEM((HD + ONES_ROWS, rows), jnp.float32),
            pltpu.VMEM((1, rows), jnp.float32),
            pltpu.VMEM((key_tile, rows), jnp.float32),
            pltpu.VMEM((key_tile, rows), jnp.float32),
            pltpu.VMEM((2, 1, rows), jnp.float32),
            pltpu.SemaphoreType.DMA((n_sems,)),
        ],
        compiler_params=params(),
        cost_estimate=cost(
            4 * n_query * rows * all_keys * HD, 4 * all_keys * HD, n_query * rows * all_keys
        ),
        name="attention",
    )(scalars, *query_pieces, *kv_pieces)


def value_blocks(values):
    count = values.shape[0]
    return jnp.swapaxes(values.reshape(count // LANES, LANES, HD), 1, 2).reshape(count, HD)


def select_rows(ids, table, clips):
    picked = jnp.broadcast_to(table[0:1], (ids.shape[0], table.shape[1]))
    for clip in range(1, clips):
        picked = jnp.where(ids == clip, table[clip : clip + 1], picked)
    return picked


def mlp_kernel(clips, n_parts, scalars, ids_ref, modulation_ref, *refs):
    parts = refs[:n_parts]
    w_in, w_out, branch, modulated = refs[n_parts:]
    step = pl.program_id(0)
    rows, width = modulated.shape

    @pl.when(step == 0)
    def _():
        part_width = width // n_parts
        mean = sum(
            jnp.sum(part[...].astype(jnp.float32), axis=1, keepdims=True) for part in parts
        ) / width
        variance = sum(
            jnp.sum((part[...].astype(jnp.float32) - mean) ** 2, axis=1, keepdims=True)
            for part in parts
        ) / width
        inverse = lax.rsqrt(variance + EPS_NORM)
        ids = ids_ref[...]
        for i, part in enumerate(parts):
            columns = pl.ds(pl.multiple_of(scalars[i] * part_width, LANES), part_width)
            normed = (part[...].astype(jnp.float32) - mean) * inverse
            shift = select_rows(ids, modulation_ref[0, :, columns], clips)
            scale = select_rows(ids, modulation_ref[1, :, columns], clips)
            modulated[:, columns] = (normed * (1.0 + scale) + shift).astype(jnp.bfloat16)

    hidden = jax.nn.gelu(
        jnp.dot(modulated[...], w_in[...], preferred_element_type=jnp.float32), approximate=True
    ).astype(jnp.bfloat16)
    product = jnp.dot(hidden, w_out[...], preferred_element_type=jnp.float32)

    @pl.when(step == 0)
    def _():
        branch[...] = product

    @pl.when(step > 0)
    def _():
        branch[...] += product


def mlp(clips, order, ids, modulation, parts, w_in, w_out):
    rows = parts[0].shape[0]
    width, units = w_in.shape
    block = math.gcd(units, 512)
    return pl.pallas_call(
        functools.partial(mlp_kernel, clips, len(parts)),
        grid=(units // block,),
        out_shape=jax.ShapeDtypeStruct((rows, width), jnp.float32),
        in_specs=[SMEM, VMEM, VMEM]
        + [VMEM] * len(parts)
        + [
            pl.BlockSpec((width, block), lambda i: (0, i)),
            pl.BlockSpec((block, width), lambda i: (i, 0)),
        ],
        out_specs=pl.BlockSpec((rows, width), lambda i: (0, 0)),
        scratch_shapes=[pltpu.VMEM((rows, width), jnp.bfloat16)],
        compiler_params=params(),
        cost_estimate=cost(4 * rows * width * units, 4 * width * units + 4 * rows * width),
        name="mlp",
    )(order, ids[:, None], modulation, *parts, w_in, w_out)


def project_kernel(heads, scalars, *refs):
    attended = refs[:heads]
    w_ref, mlp_ref, kept, sent, gathered = refs[heads:]
    share = kept.shape[0]
    for i in range(heads):
        gathered[:, pl.ds(pl.multiple_of(scalars[i] * HD, HD), HD)] = attended[i][...]
    mine = pl.ds(pl.multiple_of(scalars[heads] * share, share), share)
    other = pl.ds(pl.multiple_of(scalars[heads + 1] * share, share), share)
    kept[...] = mlp_ref[mine, :] + jnp.dot(
        gathered[mine, :], w_ref[...], preferred_element_type=jnp.float32
    )
    sent[...] = (
        mlp_ref[other, :]
        + jnp.dot(gathered[other, :], w_ref[...], preferred_element_type=jnp.float32)
    ).astype(jnp.bfloat16)


def project(scalars, attended, w_attn_out, mlp_branch):
    rows, width = mlp_branch.shape
    heads = len(attended)
    inputs = w_attn_out.shape[0]
    block = math.gcd(width, 1024)
    return pl.pallas_call(
        functools.partial(project_kernel, heads),
        grid=(width // block,),
        out_shape=[
            jax.ShapeDtypeStruct((rows // 2, width), jnp.float32),
            jax.ShapeDtypeStruct((rows // 2, width), jnp.bfloat16),
        ],
        in_specs=[SMEM]
        + [VMEM] * heads
        + [
            pl.BlockSpec((inputs, block), lambda i: (0, i)),
            pl.BlockSpec((rows, block), lambda i: (0, i)),
        ],
        out_specs=[
            pl.BlockSpec((rows // 2, block), lambda i: (0, i)),
            pl.BlockSpec((rows // 2, block), lambda i: (0, i)),
        ],
        scratch_shapes=[pltpu.VMEM((rows, inputs), jnp.bfloat16)],
        compiler_params=params(),
        cost_estimate=cost(2 * rows * width * inputs, 2 * width * inputs + 4 * rows * width),
        name="project",
    )(scalars, *attended, w_attn_out, mlp_branch)


def per_device(
    tokens,
    queries,
    key_rows,
    value_rows,
    clip_ids,
    causal,
    modulation,
    w_mlp,
    w_attn_out,
    w_mlp_out,
):
    local_rows = queries.shape[0]
    heads = queries.shape[1] // HD
    clips = causal.shape[0]
    tp_size = lax.axis_size("tp")
    ctx_size = lax.axis_size("ctx")
    here = lax.axis_index("ctx")
    tp_here = lax.axis_index("tp")
    first_row = here * local_rows
    own_ids = lax.dynamic_slice_in_dim(clip_ids, first_row, local_rows)
    clip_starts = jnp.sum(
        (clip_ids[None, :] < jnp.arange(clips + 1, dtype=jnp.int32)[:, None]).astype(jnp.int32),
        axis=1,
    )
    clip_scalars = jnp.concatenate([clip_starts, causal])
    chips = ctx_size // 2
    exchange = ctx_size % 2 == 0 and heads == chips and chips & (chips - 1) == 0
    pair = tp_size == 2

    if pair:
        other_half = lax.ppermute(tokens, "tp", [(0, 1), (1, 0)])
        parts = [tokens, other_half]
        order = jnp.stack([tp_here, 1 - tp_here])
    else:
        parts = [lax.all_gather(tokens, "tp", axis=1, tiled=True)]
        order = jnp.zeros((1,), jnp.int32)

    if exchange:
        chip, core = here // 2, here % 2
        peers = [lax.bitwise_xor(chip, k) for k in range(chips)]

        def to_chip(array, k):
            if k == 0:
                return array
            return lax.ppermute(
                array, "ctx", [(2 * i + c, 2 * (i ^ k) + c) for i in range(chips) for c in (0, 1)]
            )

        kv_sent, query_sent = split_heads(chip, chips, queries, key_rows, value_rows)
        kv_own = [to_chip(piece, k) for k, piece in enumerate(kv_sent)]
        query_pieces = [to_chip(piece, k) for k, piece in enumerate(query_sent)]
        swap = [(2 * i + c, 2 * i + 1 - c) for i in range(chips) for c in (0, 1)]
        kv_pieces = list(kv_own)
        for piece in kv_own:
            kv_pieces.append(lax.ppermute(piece, "ctx", swap))
        rows_at = [peer * (2 * local_rows) + core * local_rows for peer in peers]
        others_at = [peer * (2 * local_rows) + (1 - core) * local_rows for peer in peers]
        scalars = jnp.concatenate([clip_scalars, jnp.stack(rows_at + rows_at + others_at)])
    mlp_branch = mlp(clips, order, own_ids, modulation, parts, w_mlp, w_mlp_out)
    if exchange:
        outs = attention(clips, scalars, query_pieces, kv_pieces)
        attended = [to_chip(piece, k) for k, piece in enumerate(outs)]
        head_order = jnp.stack(peers)
    else:
        all_keys = lax.all_gather(key_rows, "ctx", axis=0, tiled=True)
        all_values = lax.all_gather(value_rows, "ctx", axis=0, tiled=True)
        scalars = jnp.concatenate([clip_scalars, jnp.stack([first_row, 0])])
        attended = []
        for head in range(heads):
            columns = slice(head * HD, (head + 1) * HD)
            kv = jnp.stack([all_keys[:, columns], value_blocks(all_values[:, columns])])
            attended.extend(attention(clips, scalars, [queries[:, columns]], [kv]))
        head_order = jnp.arange(heads, dtype=jnp.int32)

    share = local_rows // tp_size
    if pair:
        kept, sent = project(
            jnp.concatenate([head_order, order]), attended, w_attn_out, mlp_branch
        )
        arrived = lax.ppermute(sent, "tp", [(0, 1), (1, 0)])
        branch = kept + arrived.astype(jnp.float32)
    else:
        branch = lax.psum_scatter(
            mlp_branch
            + jnp.dot(
                jnp.concatenate(attended, axis=1), w_attn_out, preferred_element_type=jnp.float32
            ),
            "tp",
            scatter_dimension=0,
            tiled=True,
        )
    first_share = tp_here * share
    own = [lax.dynamic_slice_in_dim(part, first_share, share, 0) for part in parts]
    if pair:
        residual = jnp.where(
            tp_here == 0, jnp.concatenate(own, axis=1), jnp.concatenate(own[::-1], axis=1)
        )
    else:
        residual = own[0]
    share_ids = lax.dynamic_slice_in_dim(own_ids, first_share, share)
    gate_rows = select_rows(share_ids[:, None], modulation[2], clips)
    return residual.astype(jnp.float32) + gate_rows * branch


def solution(mesh):
    in_specs = (
        P("ctx", "tp"),
        P("ctx", "tp"),
        P("ctx", "tp"),
        P("ctx", "tp"),
        P(),
        P(),
        P(),
        P(None, "tp"),
        P("tp", None),
        P("tp", None),
    )
    out_specs = P(("ctx", "tp"), None)
    return jax.shard_map(
        per_device, mesh=mesh, in_specs=in_specs, out_specs=out_specs, check_vma=False
    )
```

time: 516 us -> 186 us (0.36)
  waiting for transfers between devices: 280 us -> 41.3 us
  matrix products: 127 us -> 0 us
  Pallas kernels: 0 us -> 66.5 us
  other arithmetic: 60.9 us -> 4.78 us
  starting transfers between devices: 0.13 us -> 47 us
  between operations: 13.2 us -> 0.18 us
  local copies, waits for them, and re-layouts: 31.8 us -> 23 us
    all_gather x3 -> x0, waiting for transfers between devices: 229 us -> none  [the longest x1 104 us: per_device(): value_piece = lax.all_gather(value_rows, 'ctx', axis=0, tiled=True)]
    dot_general x13 -> x0, matrix products: 127 us -> none  [the longest x4 42.6 us: attend(): jnp.einsum('hij,jhd->ihd', rounded, value_tile, preferred_element_type=jn...]
    pallas_call x0 -> x4, Pallas kernels: none -> 66.5 us  [the longest x1 29.4 us: attention(): pl.pallas_call(functools.partial(attention_kernel, clips, n_query, n_kv,...]
    reduce_scatter x1 -> x0, waiting for transfers between devices: 50.2 us -> none  [per_device(): lax.psum_scatter(jnp.dot(attended, w_attn_out, preferred_element_type=jnp...]
    reduce_sum x7 -> x1, other arithmetic: 48.3 us -> 0.16 us  [per_device(): jnp.sum((clip_ids[None, :] < jnp.arange(clips + 1, dtype=jnp.int32)[:, No...]
    ppermute x0 -> x31, starting transfers between devices: none -> 47 us  [the longest x21 43.3 us: to_chip(): lax.ppermute(array, 'ctx', [(2 * i + c, 2 * (i ^ k) + c) for i in range(c...]
    ppermute x0 -> x31, waiting for transfers between devices: none -> 41.3 us  [the longest x21 24.2 us: to_chip(): lax.ppermute(array, 'ctx', [(2 * i + c, 2 * (i ^ k) + c) for i in range(c...]
    dynamic_slice x12 -> x2, local copies, waits for them, and re-layouts: 25.6 us -> 1.15 us  [per_device(): lax.dynamic_slice_in_dim(part, first_share, share, 0)]
  transfers between devices with their start and end apart: 4 -> 31, of which waited for: 4 -> 7; matrix products, arithmetic and copies ran while one was open for 6% -> 2% of each run, Pallas kernels for 0% -> 32%
where the time goes in v1:
time: 186 us; the launch traced here: 183 us
  Pallas kernels  66.5 us (36%)
  starting transfers between devices  47 us (25%)
  waiting for transfers between devices  41.3 us (22%)
  local copies, waits for them, and re-layouts  23 us (12%)
  other arithmetic  4.78 us (3%)
    ppermute x21, starting transfers between devices, to_chip(): lax.ppermute(array, 'ctx', [(2 * i + c, 2 * (i ^ k) + c) for i in range(c...  43.3 us
    pallas_call x1, Pallas kernels, attention(): pl.pallas_call(functools.partial(attention_kernel, clips, n_query, n_kv,...  29.4 us
    pallas_call x1, Pallas kernels, mlp(): pl.pallas_call(functools.partial(mlp_kernel, clips, len(parts)), grid=(un...  28.9 us
    ppermute x21, waiting for transfers between devices, to_chip(): lax.ppermute(array, 'ctx', [(2 * i + c, 2 * (i ^ k) + c) for i in range(c...  24.2 us
    unnamed x60, local copies, waits for them, and re-layouts  20.5 us
    ppermute x1, waiting for transfers between devices, per_device(): arrived = lax.ppermute(sent, 'tp', [(0, 1), (1, 0)])  17.1 us
    pallas_call x1, Pallas kernels, project(): pl.pallas_call(functools.partial(project_kernel, heads), grid=(width // b...  7.54 us
    add x1, other arithmetic, per_device(): return residual.astype(jnp.float32) + gate_rows * branch  3.77 us
  transfers between devices with their start and end apart: 31, of which 7 were waited for; matrix products, arithmetic and copies ran while one was open for 2% of the time, Pallas kernels for 32%

profile of v1, /device:TPU:0, one launch (start us, length us, event | category | flops | bytes accessed | tf_op | source)
XLA Modules:
  0.0 182.9 jit_solution(8845828540859308061)
XLA Ops:
  4.1 3.0 %collective-permute-start.1 = (bf16[384,128]{1,0:T(8,128)(2,1)S(1)}, bf16[384,128]{1,0:T(8,128)(2,1)S(1)}, u32[]{:S(2)}, u32[]{:S(2)}) collective-permute-start(bf16[384,128]{1,0:T(8,128)(2,1)S(1)} %get-tuple-element.32), channel_id=1, source_target_pairs={{0,4},{2,6},{4,0},{6,2},{8,12},{10,14},{12,8},{14,10},{16,20},{18,... | collective-permute-start | bytes 294920 | tf_op jit(solution)/shard_map/ppermute | solution.py:378
  7.1 1.6 collective-permute-start.2
  8.7 1.9 %collective-permute-start.8 = (bf16[2,384,128]{2,1,0:T(8,128)(2,1)S(1)}, bf16[2,384,128]{2,1,0:T(8,128)(2,1)S(1)}, u32[]{:S(2)}, u32[]{:S(2)}) collective-permute-start(bf16[2,384,128]{2,1,0:T(8,128)(2,1)S(1)} %get-tuple-element.40), channel_id=1, source_target_pairs={{0,4},{2,6},{4,0},{6,2},{8,12},{10,14},{12,8},{14,10},{16,20},{18,... | collective-permute-start | bytes 589832 | tf_op jit(solution)/shard_map/ppermute | solution.py:378
  10.6 2.6 %collective-permute-start.4 = (bf16[384,128]{1,0:T(8,128)(2,1)S(1)}, bf16[384,128]{1,0:T(8,128)(2,1)S(1)}, u32[]{:S(2)}, u32[]{:S(2)}) collective-permute-start(bf16[384,128]{1,0:T(8,128)(2,1)S(1)} %get-tuple-element.35), channel_id=1, source_target_pairs={{0,16},{2,18},{4,20},{6,22},{8,24},{10,26},{12,28},{14,30},{16,0},... | collective-permute-start | bytes 294920 | tf_op jit(solution)/shard_map/ppermute | solution.py:378
  15.0 3.3 %collective-permute-start.6 = (bf16[384,128]{1,0:T(8,128)(2,1)S(1)}, bf16[384,128]{1,0:T(8,128)(2,1)S(1)}, u32[]{:S(2)}, u32[]{:S(2)}) collective-permute-start(bf16[384,128]{1,0:T(8,128)(2,1)S(1)} %get-tuple-element.37), channel_id=1, source_target_pairs={{0,24},{2,26},{4,28},{6,30},{8,16},{10,18},{12,20},{14,22},{16,8},... | collective-permute-start | bytes 294920 | tf_op jit(solution)/shard_map/ppermute | solution.py:378
  19.0 1.2 collective-permute-start.7
  20.2 3.8 %collective-permute-done.4.refs_4_ = bf16[384,128]{1,0:T(8,128)(2,1)S(1)} collective-permute-done((bf16[384,128]{1,0:T(8,128)(2,1)S(1)}, bf16[384,128]{1,0:T(8,128)(2,1)S(1)}, u32[]{:S(2)}, u32[]{:S(2)}) %collective-permute-start.4) | collective-permute-done | bytes 98336 | tf_op jit(solution)/shard_map/ppermute | solution.py:378
  28.1 4.3 %collective-permute-start.11 = (bf16[2,384,128]{2,1,0:T(8,128)(2,1)S(1)}, bf16[2,384,128]{2,1,0:T(8,128)(2,1)}, u32[]{:S(2)}, u32[]{:S(2)}) collective-permute-start(bf16[2,384,128]{2,1,0:T(8,128)(2,1)S(1)} %get-tuple-element.43), channel_id=1, source_target_pairs={{0,16},{2,18},{4,20},{6,22},{8,24},{10,26},{12,28},{14,30},{16,0},... | collective-permute-start | bytes 589832 | tf_op jit(solution)/shard_map/ppermute | solution.py:378
  33.0 2.1 %collective-permute-start.12 = (bf16[2,384,128]{2,1,0:T(8,128)(2,1)S(1)}, bf16[2,384,128]{2,1,0:T(8,128)(2,1)}, u32[]{:S(2)}, u32[]{:S(2)}) collective-permute-start(bf16[2,384,128]{2,1,0:T(8,128)(2,1)S(1)} %get-tuple-element.44), channel_id=1, source_target_pairs={{0,20},{2,22},{4,16},{6,18},{8,28},{10,30},{12,24},{14,26},{16,4},... | collective-permute-start | bytes 589832 | tf_op jit(solution)/shard_map/ppermute | solution.py:378
  36.0 2.5 %collective-permute-start.14 = (bf16[2,384,128]{2,1,0:T(8,128)(2,1)S(1)}, bf16[2,384,128]{2,1,0:T(8,128)(2,1)}, u32[]{:S(2)}, u32[]{:S(2)}) collective-permute-start(bf16[2,384,128]{2,1,0:T(8,128)(2,1)S(1)} %get-tuple-element.46), channel_id=1, source_target_pairs={{0,28},{2,30},{4,24},{6,26},{8,20},{10,22},{12,16},{14,18},{16,12}... | collective-permute-start | bytes 589832 | tf_op jit(solution)/shard_map/ppermute | solution.py:378
  38.9 16.0 %collective-permute-done.11.refs_12_ = bf16[2,384,128]{2,1,0:T(8,128)(2,1)} collective-permute-done((bf16[2,384,128]{2,1,0:T(8,128)(2,1)S(1)}, bf16[2,384,128]{2,1,0:T(8,128)(2,1)}, u32[]{:S(2)}, u32[]{:S(2)}) %collective-permute-start.11) | collective-permute-done | bytes 196640 | tf_op jit(solution)/shard_map/ppermute | solution.py:378
  54.8 3.5 %collective-permute-done.12.refs_13_ = bf16[2,384,128]{2,1,0:T(8,128)(2,1)} collective-permute-done((bf16[2,384,128]{2,1,0:T(8,128)(2,1)S(1)}, bf16[2,384,128]{2,1,0:T(8,128)(2,1)}, u32[]{:S(2)}, u32[]{:S(2)}) %collective-permute-start.12) | collective-permute-done | bytes 196640 | tf_op jit(solution)/shard_map/ppermute | solution.py:378
  62.5 1.5 collective-permute-start
  74.6 29.4 %attention.1 = (bf16[384,128]{1,0:T(8,128)(2,1)S(1)}, bf16[384,128]{1,0:T(8,128)(2,1)S(1)}, bf16[384,128]{1,0:T(8,128)(2,1)S(1)}, bf16[384,128]{1,0:T(8,128)(2,1...) custom-call(s32[33]{0:T(128)S(1)} %concatenate.16.scalars, ...), custom_call_target="tpu_custom_call" | custom-call | flops 9663676416 | bytes 3145728 | tf_op jit(solution)/shard_map/attention/pallas_call | solution.py:189
  104.1 2.2 %collective-permute-start.23 = (bf16[384,128]{1,0:T(8,128)(2,1)S(1)}, bf16[384,128]{1,0:T(8,128)(2,1)S(1)}, u32[]{:S(2)}, u32[]{:S(2)}) collective-permute-start(bf16[384,128]{1,0:T(8,128)(2,1)S(1)} %get-tuple-element.48), channel_id=1, source_target_pairs={{0,4},{2,6},{4,0},{6,2},{8,12},{10,14},{12,8},{14,10},{16,20},{18,... | collective-permute-start | bytes 294920 | tf_op jit(solution)/shard_map/ppermute | solution.py:378
  106.3 6.7 %collective-permute-start.24 = (bf16[384,128]{1,0:T(8,128)(2,1)S(1)}, bf16[384,128]{1,0:T(8,128)(2,1)S(1)}, u32[]{:S(2)}, u32[]{:S(2)}) collective-permute-start(bf16[384,128]{1,0:T(8,128)(2,1)S(1)} %get-tuple-element.49), channel_id=1, source_target_pairs={{0,8},{2,10},{4,12},{6,14},{8,0},{10,2},{12,4},{14,6},{16,24},{18,... | collective-permute-start | bytes 294920 | tf_op jit(solution)/shard_map/ppermute | solution.py:378
  113.1 2.9 %collective-permute-start.26 = (bf16[384,128]{1,0:T(8,128)(2,1)S(1)}, bf16[384,128]{1,0:T(8,128)(2,1)S(1)}, u32[]{:S(2)}, u32[]{:S(2)}) collective-permute-start(bf16[384,128]{1,0:T(8,128)(2,1)S(1)} %get-tuple-element.51), channel_id=1, source_target_pairs={{0,16},{2,18},{4,20},{6,22},{8,24},{10,26},{12,28},{14,30},{16,0},... | collective-permute-start | bytes 294920 | tf_op jit(solution)/shard_map/ppermute | solution.py:378
  116.0 1.4 collective-permute-start.27
  117.5 2.0 %collective-permute-start.28 = (bf16[384,128]{1,0:T(8,128)(2,1)S(1)}, bf16[384,128]{1,0:T(8,128)(2,1)S(1)}, u32[]{:S(2)}, u32[]{:S(2)}) collective-permute-start(bf16[384,128]{1,0:T(8,128)(2,1)S(1)} %get-tuple-element.53), channel_id=1, source_target_pairs={{0,24},{2,26},{4,28},{6,30},{8,16},{10,18},{12,20},{14,22},{16,8},... | collective-permute-start | bytes 294920 | tf_op jit(solution)/shard_map/ppermute | solution.py:378
  119.5 2.4 %collective-permute-start.29 = (bf16[384,128]{1,0:T(8,128)(2,1)S(1)}, bf16[384,128]{1,0:T(8,128)(2,1)S(1)}, u32[]{:S(2)}, u32[]{:S(2)}) collective-permute-start(bf16[384,128]{1,0:T(8,128)(2,1)S(1)} %get-tuple-element.54), channel_id=1, source_target_pairs={{0,28},{2,30},{4,24},{6,26},{8,20},{10,22},{12,16},{14,18},{16,12}... | collective-permute-start | bytes 294920 | tf_op jit(solution)/shard_map/ppermute | solution.py:378
  121.9 28.9 %mlp.1.refs_9_ = f32[384,3072]{1,0:T(8,128)} custom-call(s32[2]{0:T(128)S(1)} %pad_add_fusion.scalars, s32[384,1]{1,0:T(8,128)S(1)} %broadcast_in_dim.68.ids_ref, f32[3,4,3072]{2,1,0:T(4,128)S(1)} %copy-done.5, bf16[384,1536]{1,0:T(8,128)(2,1)S(1)} %copy-done.3, bf16[384,1536]{1,0:T(8,128)(2,1)S(1)} %collective-permute-done.refs_1_, ...), custom_call_target="tpu_custom_call" | custom-call | flops 14495514624 | bytes 42467328 | tf_op jit(solution)/shard_map/mlp/pallas_call | solution.py:269
  150.8 7.5 %project.1 = (f32[192,3072]{1,0:T(8,128)S(1)}, bf16[192,3072]{1,0:T(8,128)(2,1)}) custom-call(s32[10]{0:T(128)S(1)} %concatenate.15.scalars, bf16[384,128]{1,0:T(8,128)(2,1)S(1)} %get-tuple-element.47.refs_0_, bf16[384,128]{1,0:T(8,128)(2,1)S(1)} %collective-permute-done.23.refs_1_, bf16[384,128]{1,0:T(8,128)(2,1)S(1)} %collective-permute-done.24.refs_2_, ...), custom_call_target="tpu_custom_call" | custom-call | flops 2415919104 | bytes 11010048 | tf_op jit(solution)/shard_map/project/pallas_call | solution.py:309
  162.0 17.1 %collective-permute-done.30 = bf16[192,3072]{1,0:T(8,128)(2,1)} collective-permute-done((bf16[192,3072]{1,0:T(8,128)(2,1)}, bf16[192,3072]{1,0:T(8,128)(2,1)}, u32[]{:S(2)}, u32[]{:S(2)}) %collective-permute-start.30) | collective-permute-done | bytes 1179680 | tf_op jit(solution)/shard_map/ppermute | solution.py:413
  179.1 3.8 %multiply_add_fusion = f32[192,3072]{1,0:T(8,128)} fusion(f32[192,3072]{1,0:T(8,128)S(1)} %get-tuple-element.55, bf16[192,3072]{1,0:T(8,128)(2,1)} %collective-permute-done.30, bf16[192,1536]{1,0:T(8,128)(2,1)S(1)} %constant_dynamic-slice_fusion, bf16[192,1536]{1,0:T(8,128)(2,1)S(1)} %constant_dynamic-slice_fusion.1, f32[3072]{0:T(1024)S(1)} %bitcast.33, ...), kind=kLoop, calls=%fused_computation | loop fusion | flops 10027008 | bytes 7127617 | tf_op jit(solution)/shard_map/add | solution.py:435
  (113 shorter events, 31.2 us)
Async XLA Ops:
  4.1 9.1 %collective-permute-start.1 = (bf16[384,128]{1,0:T(8,128)(2,1)S(1)}, bf16[384,128]{1,0:T(8,128)(2,1)S(1)}, u32[]{:S(2)}, u32[]{:S(2)}) collective-permute-start(bf16[384,128]{1,0:T(8,128)(2,1)S(1)} %get-tuple-element.32), channel_id=1, source_target_pairs={{0,4},{2,6},{4,0},{6,2},{8,12},{10,14},{12,8},{14,10},{16,20},{18,... | collective-permute-start | bytes 294920 | tf_op jit(solution)/shard_map/ppermute | solution.py:378
  7.1 7.3 %collective-permute-start.2 = (bf16[384,128]{1,0:T(8,128)(2,1)S(1)}, bf16[384,128]{1,0:T(8,128)(2,1)S(1)}, u32[]{:S(2)}, u32[]{:S(2)}) collective-permute-start(bf16[384,128]{1,0:T(8,128)(2,1)S(1)} %get-tuple-element.33), channel_id=1, source_target_pairs={{0,8},{2,10},{4,12},{6,14},{8,0},{10,2},{12,4},{14,6},{16,24},{18,... | collective-permute-start | bytes 294920 | tf_op jit(solution)/shard_map/ppermute | solution.py:378
  8.7 9.7 %collective-permute-start.3 = (bf16[384,128]{1,0:T(8,128)(2,1)S(1)}, bf16[384,128]{1,0:T(8,128)(2,1)S(1)}, u32[]{:S(2)}, u32[]{:S(2)}) collective-permute-start(bf16[384,128]{1,0:T(8,128)(2,1)S(1)} %get-tuple-element.34), channel_id=1, source_target_pairs={{0,12},{2,14},{4,8},{6,10},{8,4},{10,6},{12,0},{14,2},{16,28},{18,... | collective-permute-start | bytes 294920 | tf_op jit(solution)/shard_map/ppermute | solution.py:378
  8.7 26.4 %collective-permute-start.8 = (bf16[2,384,128]{2,1,0:T(8,128)(2,1)S(1)}, bf16[2,384,128]{2,1,0:T(8,128)(2,1)S(1)}, u32[]{:S(2)}, u32[]{:S(2)}) collective-permute-start(bf16[2,384,128]{2,1,0:T(8,128)(2,1)S(1)} %get-tuple-element.40), channel_id=1, source_target_pairs={{0,4},{2,6},{4,0},{6,2},{8,12},{10,14},{12,8},{14,10},{16,20},{18,... | collective-permute-start | bytes 589832 | tf_op jit(solution)/shard_map/ppermute | solution.py:378
  10.6 13.3 %collective-permute-start.4 = (bf16[384,128]{1,0:T(8,128)(2,1)S(1)}, bf16[384,128]{1,0:T(8,128)(2,1)S(1)}, u32[]{:S(2)}, u32[]{:S(2)}) collective-permute-start(bf16[384,128]{1,0:T(8,128)(2,1)S(1)} %get-tuple-element.35), channel_id=1, source_target_pairs={{0,16},{2,18},{4,20},{6,22},{8,24},{10,26},{12,28},{14,30},{16,0},... | collective-permute-start | bytes 294920 | tf_op jit(solution)/shard_map/ppermute | solution.py:378
  13.8 12.1 %collective-permute-start.5 = (bf16[384,128]{1,0:T(8,128)(2,1)S(1)}, bf16[384,128]{1,0:T(8,128)(2,1)S(1)}, u32[]{:S(2)}, u32[]{:S(2)}) collective-permute-start(bf16[384,128]{1,0:T(8,128)(2,1)S(1)} %get-tuple-element.36), channel_id=1, source_target_pairs={{0,20},{2,22},{4,16},{6,18},{8,28},{10,30},{12,24},{14,26},{16,4},... | collective-permute-start | bytes 294920 | tf_op jit(solution)/shard_map/ppermute | solution.py:378
  15.0 12.5 %collective-permute-start.6 = (bf16[384,128]{1,0:T(8,128)(2,1)S(1)}, bf16[384,128]{1,0:T(8,128)(2,1)S(1)}, u32[]{:S(2)}, u32[]{:S(2)}) collective-permute-start(bf16[384,128]{1,0:T(8,128)(2,1)S(1)} %get-tuple-element.37), channel_id=1, source_target_pairs={{0,24},{2,26},{4,28},{6,30},{8,16},{10,18},{12,20},{14,22},{16,8},... | collective-permute-start | bytes 294920 | tf_op jit(solution)/shard_map/ppermute | solution.py:378
  19.0 13.4 %collective-permute-start.7 = (bf16[384,128]{1,0:T(8,128)(2,1)S(1)}, bf16[384,128]{1,0:T(8,128)(2,1)S(1)}, u32[]{:S(2)}, u32[]{:S(2)}) collective-permute-start(bf16[384,128]{1,0:T(8,128)(2,1)S(1)} %get-tuple-element.38), channel_id=1, source_target_pairs={{0,28},{2,30},{4,24},{6,26},{8,20},{10,22},{12,16},{14,18},{16,12}... | collective-permute-start | bytes 294920 | tf_op jit(solution)/shard_map/ppermute | solution.py:378
  24.6 11.4 %collective-permute-start.9 = (bf16[2,384,128]{2,1,0:T(8,128)(2,1)S(1)}, bf16[2,384,128]{2,1,0:T(8,128)(2,1)S(1)}, u32[]{:S(2)}, u32[]{:S(2)}) collective-permute-start(bf16[2,384,128]{2,1,0:T(8,128)(2,1)S(1)} %get-tuple-element.41), channel_id=1, source_target_pairs={{0,8},{2,10},{4,12},{6,14},{8,0},{10,2},{12,4},{14,6},{16,24},{18,... | collective-permute-start | bytes 589832 | tf_op jit(solution)/shard_map/ppermute | solution.py:378
  26.6 12.3 %collective-permute-start.10 = (bf16[2,384,128]{2,1,0:T(8,128)(2,1)S(1)}, bf16[2,384,128]{2,1,0:T(8,128)(2,1)S(1)}, u32[]{:S(2)}, u32[]{:S(2)}) collective-permute-start(bf16[2,384,128]{2,1,0:T(8,128)(2,1)S(1)} %get-tuple-element.42), channel_id=1, source_target_pairs={{0,12},{2,14},{4,8},{6,10},{8,4},{10,6},{12,0},{14,2},{16,28},{18,... | collective-permute-start | bytes 589832 | tf_op jit(solution)/shard_map/ppermute | solution.py:378
  28.1 26.7 %collective-permute-start.11 = (bf16[2,384,128]{2,1,0:T(8,128)(2,1)S(1)}, bf16[2,384,128]{2,1,0:T(8,128)(2,1)}, u32[]{:S(2)}, u32[]{:S(2)}) collective-permute-start(bf16[2,384,128]{2,1,0:T(8,128)(2,1)S(1)} %get-tuple-element.43), channel_id=1, source_target_pairs={{0,16},{2,18},{4,20},{6,22},{8,24},{10,26},{12,28},{14,30},{16,0},... | collective-permute-start | bytes 589832 | tf_op jit(solution)/shard_map/ppermute | solution.py:378
  33.0 25.2 %collective-permute-start.12 = (bf16[2,384,128]{2,1,0:T(8,128)(2,1)S(1)}, bf16[2,384,128]{2,1,0:T(8,128)(2,1)}, u32[]{:S(2)}, u32[]{:S(2)}) collective-permute-start(bf16[2,384,128]{2,1,0:T(8,128)(2,1)S(1)} %get-tuple-element.44), channel_id=1, source_target_pairs={{0,20},{2,22},{4,16},{6,18},{8,28},{10,30},{12,24},{14,26},{16,4},... | collective-permute-start | bytes 589832 | tf_op jit(solution)/shard_map/ppermute | solution.py:378
  35.1 23.2 %collective-permute-start.13 = (bf16[2,384,128]{2,1,0:T(8,128)(2,1)S(1)}, bf16[2,384,128]{2,1,0:T(8,128)(2,1)}, u32[]{:S(2)}, u32[]{:S(2)}) collective-permute-start(bf16[2,384,128]{2,1,0:T(8,128)(2,1)S(1)} %get-tuple-element.45), channel_id=1, source_target_pairs={{0,24},{2,26},{4,28},{6,30},{8,16},{10,18},{12,20},{14,22},{16,8},... | collective-permute-start | bytes 589832 | tf_op jit(solution)/shard_map/ppermute | solution.py:378
  36.0 22.8 %collective-permute-start.14 = (bf16[2,384,128]{2,1,0:T(8,128)(2,1)S(1)}, bf16[2,384,128]{2,1,0:T(8,128)(2,1)}, u32[]{:S(2)}, u32[]{:S(2)}) collective-permute-start(bf16[2,384,128]{2,1,0:T(8,128)(2,1)S(1)} %get-tuple-element.46), channel_id=1, source_target_pairs={{0,28},{2,30},{4,24},{6,26},{8,20},{10,22},{12,16},{14,18},{16,12}... | collective-permute-start | bytes 589832 | tf_op jit(solution)/shard_map/ppermute | solution.py:378
  38.9 20.0 %collective-permute-start.15 = (bf16[2,384,128]{2,1,0:T(8,128)(2,1)S(1)}, bf16[2,384,128]{2,1,0:T(8,128)(2,1)S(1)}, u32[]{:S(2)}, u32[]{:S(2)}) collective-permute-start(bf16[2,384,128]{2,1,0:T(8,128)(2,1)S(1)} %get-tuple-element.39.refs_8_), channel_id=1, source_target_pairs={{0,2},{2,0},{4,6},{6,4},{8,10},{10,8},{12,14},{14,12},{16,18},{18,... | collective-permute-start | bytes 589832 | tf_op jit(solution)/shard_map/ppermute | solution.py:388
  62.5 56.9 %collective-permute-start = (bf16[384,1536]{1,0:T(8,128)(2,1)S(1)}, bf16[384,1536]{1,0:T(8,128)(2,1)S(1)}, u32[]{:S(2)}, u32[]{:S(2)}) collective-permute-start(bf16[384,1536]{1,0:T(8,128)(2,1)S(1)} %copy-done.3), channel_id=1, source_target_pairs={{0,1},{1,0},{2,3},{3,2},{4,5},{5,4},{6,7},{7,6},{8,9},{9,8},{10,11... | collective-permute-start | bytes 3538952 | tf_op jit(solution)/shard_map/ppermute | solution.py:364
  104.1 12.0 %collective-permute-start.23 = (bf16[384,128]{1,0:T(8,128)(2,1)S(1)}, bf16[384,128]{1,0:T(8,128)(2,1)S(1)}, u32[]{:S(2)}, u32[]{:S(2)}) collective-permute-start(bf16[384,128]{1,0:T(8,128)(2,1)S(1)} %get-tuple-element.48), channel_id=1, source_target_pairs={{0,4},{2,6},{4,0},{6,2},{8,12},{10,14},{12,8},{14,10},{16,20},{18,... | collective-permute-start | bytes 294920 | tf_op jit(solution)/shard_map/ppermute | solution.py:378
  106.3 11.2 %collective-permute-start.24 = (bf16[384,128]{1,0:T(8,128)(2,1)S(1)}, bf16[384,128]{1,0:T(8,128)(2,1)S(1)}, u32[]{:S(2)}, u32[]{:S(2)}) collective-permute-start(bf16[384,128]{1,0:T(8,128)(2,1)S(1)} %get-tuple-element.49), channel_id=1, source_target_pairs={{0,8},{2,10},{4,12},{6,14},{8,0},{10,2},{12,4},{14,6},{16,24},{18,... | collective-permute-start | bytes 294920 | tf_op jit(solution)/shard_map/ppermute | solution.py:378
  113.1 37.7 %collective-permute-start.25 = (bf16[384,128]{1,0:T(8,128)(2,1)S(1)}, bf16[384,128]{1,0:T(8,128)(2,1)S(1)}, u32[]{:S(2)}, u32[]{:S(2)}) collective-permute-start(bf16[384,128]{1,0:T(8,128)(2,1)S(1)} %get-tuple-element.50), channel_id=1, source_target_pairs={{0,12},{2,14},{4,8},{6,10},{8,4},{10,6},{12,0},{14,2},{16,28},{18,... | collective-permute-start | bytes 294920 | tf_op jit(solution)/shard_map/ppermute | solution.py:378
  113.1 37.6 %collective-permute-start.26 = (bf16[384,128]{1,0:T(8,128)(2,1)S(1)}, bf16[384,128]{1,0:T(8,128)(2,1)S(1)}, u32[]{:S(2)}, u32[]{:S(2)}) collective-permute-start(bf16[384,128]{1,0:T(8,128)(2,1)S(1)} %get-tuple-element.51), channel_id=1, source_target_pairs={{0,16},{2,18},{4,20},{6,22},{8,24},{10,26},{12,28},{14,30},{16,0},... | collective-permute-start | bytes 294920 | tf_op jit(solution)/shard_map/ppermute | solution.py:378
  116.0 34.7 %collective-permute-start.27 = (bf16[384,128]{1,0:T(8,128)(2,1)S(1)}, bf16[384,128]{1,0:T(8,128)(2,1)S(1)}, u32[]{:S(2)}, u32[]{:S(2)}) collective-permute-start(bf16[384,128]{1,0:T(8,128)(2,1)S(1)} %get-tuple-element.52), channel_id=1, source_target_pairs={{0,20},{2,22},{4,16},{6,18},{8,28},{10,30},{12,24},{14,26},{16,4},... | collective-permute-start | bytes 294920 | tf_op jit(solution)/shard_map/ppermute | solution.py:378
  117.5 33.3 %collective-permute-start.28 = (bf16[384,128]{1,0:T(8,128)(2,1)S(1)}, bf16[384,128]{1,0:T(8,128)(2,1)S(1)}, u32[]{:S(2)}, u32[]{:S(2)}) collective-permute-start(bf16[384,128]{1,0:T(8,128)(2,1)S(1)} %get-tuple-element.53), channel_id=1, source_target_pairs={{0,24},{2,26},{4,28},{6,30},{8,16},{10,18},{12,20},{14,22},{16,8},... | collective-permute-start | bytes 294920 | tf_op jit(solution)/shard_map/ppermute | solution.py:378
  119.5 31.3 %collective-permute-start.29 = (bf16[384,128]{1,0:T(8,128)(2,1)S(1)}, bf16[384,128]{1,0:T(8,128)(2,1)S(1)}, u32[]{:S(2)}, u32[]{:S(2)}) collective-permute-start(bf16[384,128]{1,0:T(8,128)(2,1)S(1)} %get-tuple-element.54), channel_id=1, source_target_pairs={{0,28},{2,30},{4,24},{6,26},{8,20},{10,22},{12,16},{14,18},{16,12}... | collective-permute-start | bytes 294920 | tf_op jit(solution)/shard_map/ppermute | solution.py:378
  158.4 20.8 %collective-permute-start.30 = (bf16[192,3072]{1,0:T(8,128)(2,1)}, bf16[192,3072]{1,0:T(8,128)(2,1)}, u32[]{:S(2)}, u32[]{:S(2)}) collective-permute-start(bf16[192,3072]{1,0:T(8,128)(2,1)} %get-tuple-element.56), channel_id=1, source_target_pairs={{0,1},{1,0},{2,3},{3,2},{4,5},{5,4},{6,7},{7,6},{8,9},{9,8},{10,11... | collective-permute-start | bytes 3538952 | tf_op jit(solution)/shard_map/ppermute | solution.py:413
  (37 other events, 316.1 us)
